TPU v7x, 512 devices: a whole 4x8x8 slice. The times are simulated.
512 devices in a mesh: ctx: 128 (over z, x, y_lo, core), head: 4 (over y_hi).
Axes of the slice: x: 4, y: 8 (y_hi: 4, y_lo: 2; y = y_hi * 2 + y_lo), z: 8, core: 2. Of those that a mesh axis runs over, the one named last changes fastest.
Arguments:
- hidden: bfloat16 [10240, 2048], P('ctx'), may hold values from -6 to 6
- self_gain: float32 [2048], replicated, may hold values from 0.5 to 8, as said below
- cross_gain: float32 [2048], replicated, may hold values from 0.5 to 8, as said below
- self_query: bfloat16 [2048, 1024], P(None, 'head'), may hold values from -0.0625 to 0.0625
- self_key: bfloat16 [2048, 1024], P(None, 'head'), may hold values from -0.125 to 0.125
- self_value: bfloat16 [2048, 1024], P(None, 'head'), may hold values from -0.125 to 0.125
- self_out: bfloat16 [2048, 1024], P(None, 'head'), may hold values from -0.1875 to 0.1875
- cross_query: bfloat16 [2048, 1024], P('ctx', 'head'), may hold values from -0.0625 to 0.0625
- cross_out: bfloat16 [2048, 1024], P('ctx', 'head'), may hold values from -0.1875 to 0.1875
- enc_key: bfloat16 [2048, 1024], P('ctx', 'head'), may hold values from -6 to 6
- enc_value: bfloat16 [2048, 1024], P('ctx', 'head'), may hold values from -6 to 6
Outputs:
- layer_out: bfloat16 [10240, 2048], P('ctx', 'head')
Inputs may be any that keep to these rules, and one draw needn't show every extreme that they name: `self_gain`: positive norm gains. `cross_gain`: positive norm gains.
All inputs are finite; a program needn't handle non-finite values.
Results may differ from a plain program's by a relative error of at most 0.03.
The roundings to bfloat16 on the way count: a program that leaves them out, or rounds other values in their place, can miss the bound.
Values may be sent and summed in bfloat16 or wider, within the bound.
A program may use at most 128 MiB of HBM per device.

v0:
```python
import jax
import jax.numpy as jnp
from jax import lax
from jax.sharding import PartitionSpec as P

KV = 64


epsilon = 1e-06


def rms_scale(vector, gain_vector):
    mean_square = jnp.mean(vector * vector, axis=-1, keepdims=True)
    return vector * lax.rsqrt(mean_square + epsilon) * gain_vector


def fold_piece(state_now, shaped_queries, pieces, query_pos, causal):
    running, peak_score, weight_sum = state_now
    key_piece, value_piece = pieces
    key_count = key_piece.shape[0]
    head_count = shaped_queries.shape[1]
    key_heads = key_piece.reshape(key_count, head_count, KV)
    value_heads = value_piece.reshape(key_count, head_count, KV)
    scores = jnp.einsum(
        "qhd,khd->hqk", shaped_queries, key_heads, preferred_element_type=jnp.float32
    )
    if causal:
        key_pos = jnp.arange(key_count, dtype=jnp.int32)
        visible = key_pos[None, None, :] <= query_pos[None, :, None]
        scores = jnp.where(visible, scores, jnp.float32(-1e30))
    new_peak = jnp.maximum(peak_score, jnp.max(scores, axis=2, keepdims=True))
    weights = jnp.exp(scores - new_peak)
    if causal:
        weights = jnp.where(visible, weights, jnp.float32(0.0))
    weight_sum = jnp.sum(weights, axis=2, keepdims=True)
    update = jnp.einsum(
        "hqk,khd->hqd",
        weights.astype(jnp.bfloat16),
        value_heads,
        preferred_element_type=jnp.float32,
    )
    return (update, new_peak, weight_sum)


def finish_heads(state_now):
    running, peak_score, weight_sum = state_now
    result = running / weight_sum
    head_count, row_count, _ = result.shape
    return jnp.transpose(result, (1, 0, 2)).reshape(row_count, head_count * KV).astype(jnp.bfloat16)


def fresh_state(head_count, row_count):
    return (
        jnp.zeros((head_count, row_count, KV), jnp.float32),
        jnp.full((head_count, row_count, 1), -1e30, jnp.float32),
        jnp.zeros((head_count, row_count, 1), jnp.float32),
    )


def body(
    hidden,
    self_gain,
    cross_gain,
    self_query,
    self_key,
    self_value,
    self_out,
    cross_query,
    cross_out,
    enc_key,
    enc_value,
):
    row_count = hidden.shape[0]
    width = hidden.shape[1]
    head_count = self_query.shape[1] // KV
    inputs = hidden.astype(jnp.float32)
    normed = rms_scale(inputs, self_gain).astype(jnp.bfloat16)
    queries = jnp.dot(normed, self_query, preferred_element_type=jnp.float32).astype(jnp.bfloat16)
    key_rows = jnp.dot(normed, self_key, preferred_element_type=jnp.float32).astype(jnp.bfloat16)
    value_rows = jnp.dot(normed, self_value, preferred_element_type=jnp.float32).astype(
        jnp.bfloat16
    )
    ctx_index = lax.axis_index("ctx")
    query_pos = ctx_index * row_count + jnp.arange(row_count, dtype=jnp.int32)
    shaped_self = queries.reshape(row_count, head_count, KV)
    start_state = fresh_state(head_count, row_count)
    final_state = fold_piece(
        start_state,
        shaped_self,
        (
            lax.all_gather(key_rows, "ctx", axis=0, tiled=True),
            lax.all_gather(value_rows, "ctx", axis=0, tiled=True),
        ),
        query_pos,
        True,
    )
    attn_self = finish_heads(final_state)
    partial_terms = lax.dot_general(
        attn_self, self_out, (((1,), (1,)), ((), ())), preferred_element_type=jnp.float32
    )
    share = width // lax.axis_size("head")
    column_start = lax.axis_index("head") * share
    summed = lax.psum(partial_terms.astype(jnp.bfloat16), "head").astype(jnp.float32)
    mixed_rows = inputs + summed
    normed2 = rms_scale(mixed_rows, cross_gain).astype(jnp.bfloat16)
    mixed_share = lax.dynamic_slice_in_dim(mixed_rows, column_start, share, 1)
    whole_query, whole_out = (
        lax.all_gather(cross_query, "ctx", axis=0, tiled=True),
        lax.all_gather(cross_out, "ctx", axis=0, tiled=True),
    )
    cross_q = jnp.dot(normed2, whole_query, preferred_element_type=jnp.float32).astype(jnp.bfloat16)
    shaped_cross = cross_q.reshape(row_count, head_count, KV)
    cross_state = fold_piece(
        fresh_state(head_count, row_count),
        shaped_cross,
        (
            lax.all_gather(enc_key, "ctx", axis=0, tiled=True),
            lax.all_gather(enc_value, "ctx", axis=0, tiled=True),
        ),
        query_pos,
        False,
    )
    attn_cross = finish_heads(cross_state)
    out_partial = lax.dot_general(
        attn_cross, whole_out, (((1,), (1,)), ((), ())), preferred_element_type=jnp.float32
    )
    out_share = lax.psum_scatter(
        out_partial.astype(jnp.bfloat16), "head", scatter_dimension=1, tiled=True
    ).astype(jnp.float32)
    return (mixed_share + out_share).astype(jnp.bfloat16)


def solution(mesh):
    placed = (
        P("ctx", None),
        P(),
        P(),
        P(None, "head"),
        P(None, "head"),
        P(None, "head"),
        P(None, "head"),
        P("ctx", "head"),
        P("ctx", "head"),
        P("ctx", "head"),
        P("ctx", "head"),
    )
    return jax.shard_map(
        body, mesh=mesh, in_specs=placed, out_specs=P("ctx", "head"), check_vma=False
    )
```

profile of v0, /device:TPU:1, one launch (start us, length us, event | category | flops | bytes accessed | tf_op | source)
XLA Modules:
  0.0 1410.2 jit_solution(17395878318094756547)
XLA Ops:
  6.5 1.2 fusion.30
  7.8 2.3 convolution_convert_fusion.4
  10.2 2.3 convolution_convert_fusion.3
  14.4 1.7 convolution_convert_fusion.5
  16.2 220.0 %all-gather.7.cloned.1.call-done = bf16[10240,256]{1,0:T(8,128)(2,1)} async-done(((bf16[80,256]{1,0:T(8,128)(2,1)}), bf16[10240,256]{1,0:T(8,128)(2,1)}) %all-gather.7.cloned.1.call-update) | async-done | bytes 5242896 | tf_op jit(solution)/shard_map/all_gather | solution.py:91
  236.3 8.0 copy.19
  244.2 9.5 fusion.39
  253.8 204.4 %all-gather.9.cloned.1.call-done = bf16[10240,256]{1,0:T(8,128)(2,1)} async-done(((bf16[80,256]{1,0:T(8,128)(2,1)}), bf16[10240,256]{1,0:T(8,128)(2,1)}) %all-gather.9.cloned.1.call-update) | async-done | bytes 5242896 | tf_op jit(solution)/shard_map/all_gather | solution.py:92
  458.2 8.0 copy.20
  466.2 7.8 fusion
  473.9 8.9 fusion.27
  482.9 1.2 convolution_convert_fusion.1
  485.6 186.4 %all-gather.13.cloned.1.call-done = bf16[2048,256]{1,0:T(8,128)(2,1)} async-done(((bf16[16,256]{1,0:T(8,128)(2,1)}), bf16[2048,256]{1,0:T(8,128)(2,1)}) %all-gather.13.cloned.1.call-update) | async-done | bytes 1048592 | tf_op jit(solution)/shard_map/all_gather | solution.py:117
  672.0 1.5 copy.22
  673.5 212.5 %all-gather.15.cloned.1.call-done = bf16[2048,256]{1,0:T(8,128)(2,1)} async-done(((bf16[16,256]{1,0:T(8,128)(2,1)}), bf16[2048,256]{1,0:T(8,128)(2,1)}) %all-gather.15.cloned.1.call-update) | async-done | bytes 1048592 | tf_op jit(solution)/shard_map/all_gather | solution.py:118
  886.0 1.5 copy.23
  887.5 55.6 %all-reduce.2.cloned.1.call-done = bf16[80,2048]{1,0:T(8,128)(2,1)} async-done(((bf16[80,2048]{1,0:T(8,128)(2,1)}), bf16[80,2048]{1,0:T(8,128)(2,1)}) %all-reduce.2.cloned.1.call-update) | async-done | bytes 327696 | tf_op jit(solution)/shard_map/psum | solution.py:103
  943.1 2.0 convert_add_fusion
  945.2 213.6 %all-gather.11.cloned.1.call-done = bf16[2048,256]{1,0:T(8,128)(2,1)} async-done(((bf16[16,256]{1,0:T(8,128)(2,1)}), bf16[2048,256]{1,0:T(8,128)(2,1)}) %all-gather.11.cloned.1.call-update) | async-done | bytes 1048592 | tf_op jit(solution)/shard_map/all_gather | solution.py:108
  1158.8 1.7 convolution_convert_fusion.2
  1162.4 210.6 %all-gather.17.cloned.1.call-done = bf16[2048,256]{1,0:T(8,128)(2,1)} async-done(((bf16[16,256]{1,0:T(8,128)(2,1)}), bf16[2048,256]{1,0:T(8,128)(2,1)}) %all-gather.17.cloned.1.call-update) | async-done | bytes 1048592 | tf_op jit(solution)/shard_map/all_gather | solution.py:109
  1373.0 2.4 convolution_convert_fusion
  1375.4 26.4 %reduce-scatter.2.cloned.1.call-done = bf16[80,512]{1,0:T(8,128)(2,1)} async-done(((bf16[80,2048]{1,0:T(8,128)(2,1)}), bf16[80,512]{1,0:T(8,128)(2,1)}) %reduce-scatter.2.cloned.1.call-update) | async-done | bytes 81936 | tf_op jit(solution)/shard_map/reduce_scatter | solution.py:127
  1401.8 1.6 add_convert_fusion
  (33 shorter events, 5.5 us)
Async XLA Ops:
  6.5 476.3 %copy-start = (bf16[2048,256]{1,0:T(8,128)(2,1)S(1)}, bf16[2048,256]{1,0:T(8,128)(2,1)}, u32[]{:S(2)}) copy-start(bf16[2048,256]{1,0:T(8,128)(2,1)} %param.17) | copy-start | bytes 3145732
  6.5 229.7 %all-gather.7.cloned.1.call-start = ((), (), s32[]{:S(2)}) async-start(), calls=%async_computation.1 | async-start | bytes 5283840 | tf_op jit(solution)/shard_map/all_gather | solution.py:91
  10.1 448.1 %all-gather.9.cloned.1.call-start = ((), (), s32[]{:S(2)}) async-start(), calls=%async_computation.2 | async-start | bytes 5283840 | tf_op jit(solution)/shard_map/all_gather | solution.py:92
  12.5 659.5 %all-gather.13.cloned.1.call-start = ((), (), s32[]{:S(2)}) async-start(), calls=%async_computation.5 | async-start | bytes 1056768 | tf_op jit(solution)/shard_map/all_gather | solution.py:117
  13.3 872.8 %all-gather.15.cloned.1.call-start = ((), (), s32[]{:S(2)}) async-start(), calls=%async_computation.6 | async-start | bytes 1056768 | tf_op jit(solution)/shard_map/all_gather | solution.py:118
  13.8 929.3 %all-reduce.2.cloned.1.call-start = ((), (), s32[]{:S(2)}) async-start(), calls=%async_computation.3 | async-start | bytes 655360 | tf_op jit(solution)/shard_map/psum | solution.py:103
  482.8 460.3 %copy-start.1 = (bf16[80,2048]{1,0:T(8,128)(2,1)S(1)}, bf16[80,2048]{1,0:T(8,128)(2,1)}, u32[]{:S(2)}) copy-start(bf16[80,2048]{1,0:T(8,128)(2,1)} %param.11) | copy-start | bytes 983044
  482.9 675.9 %copy-start.2 = (f32[2048]{0:T(1024)S(1)}, f32[2048]{0:T(1024)}, u32[]{:S(2)}) copy-start(f32[2048]{0:T(1024)} %param.13) | copy-start | bytes 24580
  484.1 674.7 %all-gather.11.cloned.1.call-start = ((), (), s32[]{:S(2)}) async-start(), calls=%async_computation.4 | async-start | bytes 1056768 | tf_op jit(solution)/shard_map/all_gather | solution.py:108
  484.7 888.3 %all-gather.17.cloned.1.call-start = ((), (), s32[]{:S(2)}) async-start(), calls=%async_computation.7 | async-start | bytes 1056768 | tf_op jit(solution)/shard_map/all_gather | solution.py:109
  485.4 916.4 %reduce-scatter.2.cloned.1.call-start = ((), (), s32[]{:S(2)}) async-start(), calls=%async_computation.8 | async-start | bytes 409600 | tf_op jit(solution)/shard_map/reduce_scatter | solution.py:127
Sparse Core Ops, SparseCore 0:
  10.2 225.9 all-gather.6
  238.4 219.7 all-gather.8
  460.4 211.5 all-gather.12
  674.0 211.9 all-gather.14
  888.8 54.2 all-reduce.1
  945.1 213.5 all-gather.10
  1160.9 211.9 all-gather.16
  1375.8 25.9 reduce-scatter.1
where the time goes:
time: 1410 us
  waiting for transfers between devices  1330 us (94%)
  matrix products  31.3 us (2%)
  local copies, waits for them, and re-layouts  19.2 us (1%)
    all_gather x1, waiting for transfers between devices, body(): lax.all_gather(key_rows, 'ctx', axis=0, tiled=True)  220 us
    all_gather x1, waiting for transfers between devices, body(): lax.all_gather(cross_query, 'ctx', axis=0, tiled=True)  214 us
    all_gather x1, waiting for transfers between devices, body(): lax.all_gather(enc_value, 'ctx', axis=0, tiled=True)  213 us
    all_gather x1, waiting for transfers between devices, body(): lax.all_gather(cross_out, 'ctx', axis=0, tiled=True)  211 us
    all_gather x1, waiting for transfers between devices, body(): lax.all_gather(value_rows, 'ctx', axis=0, tiled=True)  204 us
    all_gather x1, waiting for transfers between devices, body(): lax.all_gather(enc_key, 'ctx', axis=0, tiled=True)  186 us
    psum x1, waiting for transfers between devices, body(): lax.psum(partial_terms.astype(jnp.bfloat16), 'head').astype(jnp.float32)  55.6 us
  transfers between devices with their start and end apart: 8, of which 8 were waited for; matrix products, arithmetic and copies ran while one was open for 4% of the time, Pallas kernels for 0%

commit v1 on v0

v1 whole, which is shorter than its diff:
```python
import functools

import jax
import jax.numpy as jnp
from jax import lax
from jax.experimental import pallas as pl
from jax.experimental.pallas import tpu as pltpu
from jax.sharding import PartitionSpec as P

KV = 64
CORES = 2
PLANE = 16
MESH = pl.DeviceIdType.MESH

epsilon = 1e-06

NT = (((1,), (1,)), ((), ()))
NN = (((1,), (0,)), ((), ()))


def matmul(left, right, dims=NN):
    return lax.dot_general(left, right, dims, preferred_element_type=jnp.float32)


def to_lanes(columns):
    rows = columns.shape[0]
    square = jnp.concatenate([columns, jnp.zeros((128 - rows, 128), jnp.float32)], axis=0)
    return jnp.transpose(square)[:8]


def to_columns(lanes, rows):
    square = jnp.concatenate([lanes, jnp.zeros((120, 128), jnp.float32)], axis=0)
    return jnp.transpose(square)[:rows]


def spread(per_head, width):
    rows = per_head.shape[0]
    owner = lax.broadcasted_iota(jnp.int32, (rows, width), 1) // KV
    result = jnp.zeros((rows, width), jnp.float32)
    for head in range(width // KV):
        result = jnp.where(owner == head, per_head[:, head : head + 1], result)
    return result


def attend(queries, keys, values, first_query):
    rows, width = queries.shape
    heads = width // KV
    owner = lax.broadcasted_iota(jnp.int32, (rows, width), 1) // KV
    zero = jnp.zeros_like(queries)
    stacked = jnp.concatenate(
        [jnp.where(owner == head, queries, zero) for head in range(heads)], axis=0
    )
    scores = matmul(stacked, keys, NT)
    if first_query is not None:
        token = lax.broadcasted_iota(jnp.int32, (rows, scores.shape[1]), 0) + first_query
        seen = lax.broadcasted_iota(jnp.int32, (rows, scores.shape[1]), 1) <= token
        scores = jnp.where(
            jnp.concatenate([seen] * heads, axis=0), scores, jnp.float32(-1e30)
        )
    peak = jnp.max(scores, axis=1, keepdims=True)
    weights = jnp.exp(scores - peak)
    total = jnp.sum(weights, axis=1, keepdims=True)
    mixed = matmul(weights.astype(jnp.bfloat16), values)
    mixed = mixed / total
    level = peak + jnp.log(total)
    result = jnp.zeros((rows, width), jnp.float32)
    levels = jnp.zeros((rows, 128), jnp.float32)
    column = lax.broadcasted_iota(jnp.int32, (rows, 128), 1)
    for head in range(heads):
        part = slice(head * rows, (head + 1) * rows)
        result = jnp.where(owner == head, mixed[part], result)
        levels = jnp.where(column == head, level[part], levels)
    return result, levels


def kernel(
    planes,
    plane_size,
    head_devices,
    hidden,
    self_gain,
    cross_gain,
    self_query,
    self_key,
    self_value,
    self_out,
    enc_key,
    enc_value,
    cross_query,
    cross_out,
    out,
    weights,
    normed,
    kv,
    qs,
    sent_part,
    sent_level,
    got_part,
    got_level,
    own_part,
    own_level,
    side,
    out_terms,
    got_terms,
    shares,
    squares,
    final_terms,
    got_final,
    load_sem,
    kv_send,
    kv_recv,
    side_z_send,
    side_z_recv,
    side_send,
    side_recv,
    q_send,
    q_recv,
    part_send,
    part_recv,
    level_send,
    level_recv,
    terms_send,
    terms_recv,
    share_send,
    share_recv,
    square_send,
    square_recv,
    final_send,
    final_recv,
):
    rows, width = hidden.shape
    share = width // head_devices
    chips = plane_size // CORES
    ctx = lax.axis_index("ctx")
    head = lax.axis_index("head")
    plane = ctx // plane_size
    place = ctx % plane_size
    chip = place // CORES
    core = place % CORES
    sibling_place = chip * CORES + (1 - core)

    def in_plane(other_place):
        return (plane * plane_size + other_place, head)

    def on_line(other_plane):
        return (other_plane * plane_size + place, head)

    def chip_place(step):
        return ((chip + step) % chips) * CORES + core

    def line_plane(step):
        return (plane + step) % planes

    def head_at(step):
        return (head + step) % head_devices

    def remote(src, dst, send, recv, device):
        return pltpu.make_async_remote_copy(
            src_ref=src,
            dst_ref=dst,
            send_sem=send,
            recv_sem=recv,
            device_id=device,
            device_id_type=MESH,
        )

    def each(low, high, step_fn):
        def step(index, carry):
            step_fn(index)
            return carry

        lax.fori_loop(low, high, step, 0)

    barrier = pltpu.get_barrier_semaphore()

    def greet(device):
        pl.semaphore_signal(barrier, inc=1, device_id=device, device_id_type=MESH)

    each(1, chips, lambda step: greet(in_plane(chip_place(step))))
    greet(in_plane(sibling_place))
    each(1, planes, lambda step: greet(on_line(line_plane(step))))
    each(1, head_devices, lambda step: greet((ctx, head_at(step))))

    loads = [
        pltpu.make_async_copy(source, weights.at[index], load_sem.at[index])
        for index, source in enumerate((self_key, self_value, self_query, self_out))
    ]
    for load in loads:
        load.start()
    for index, source in enumerate((enc_key, enc_value, cross_query, cross_out)):
        side[index, plane, place] = source[...]

    pl.semaphore_wait(barrier, (chips - 1) + 1 + (planes - 1) + (head_devices - 1))

    def side_line(step, other):
        block = side.at[:, other, place]
        return remote(
            block, block, side_z_send.at[step], side_z_recv.at[other], on_line(line_plane(step))
        )

    each(1, planes, lambda step: side_line(step, plane).start())

    inputs = hidden[...].astype(jnp.float32)
    mean_square = jnp.mean(inputs * inputs, axis=1, keepdims=True)
    normed[...] = (inputs * lax.rsqrt(mean_square + epsilon) * self_gain[...]).astype(jnp.bfloat16)

    for index in range(2):
        loads[index].wait()
        kv[index, place] = matmul(normed[...], weights[index]).astype(jnp.bfloat16)

    def spread_copy(buffer, send, recv):
        def copy(slot, sender, device):
            return remote(buffer(slot), buffer(slot), send.at[sender], recv.at[slot], device)

        def start():
            each(1, chips, lambda step: copy(place, step, in_plane(chip_place(step))).start())
            copy(place, 0, in_plane(sibling_place)).start()

        def forward():
            def one(step):
                slot = chip_place(step)
                copy(slot, chips + step, in_plane(sibling_place)).wait_recv()
                copy(slot, chips + step, in_plane(sibling_place)).start()

            each(1, chips, one)

        def finish():
            def one(step):
                slot = ((chip + step) % chips) * CORES + (1 - core)
                copy(slot, 0, in_plane(sibling_place)).wait_recv()

            each(0, chips, one)

        def drain():
            def one(step):
                copy(place, step, in_plane(sibling_place)).wait_send()

            each(0, chips, one)
            each(chips + 1, 2 * chips, one)

        return start, forward, finish, drain

    kv_start, kv_forward, kv_finish, kv_drain = spread_copy(
        lambda slot: kv.at[:, slot], kv_send, kv_recv
    )
    side_start, side_forward, side_finish, side_drain = spread_copy(
        lambda slot: side.at[:, :, slot], side_send, side_recv
    )
    kv_start()

    loads[2].wait()
    qs[plane] = matmul(normed[...], weights[2]).astype(jnp.bfloat16)

    def query_copy(source_plane, target_plane):
        return remote(
            qs.at[source_plane],
            qs.at[source_plane],
            q_send.at[target_plane],
            q_recv.at[source_plane],
            on_line(target_plane),
        )

    each(0, plane, lambda target: query_copy(plane, target).start())

    def side_arrival(step):
        side_line(step, line_plane(step)).wait_recv()

    each(1, planes, side_arrival)
    side_start()

    kv_forward()
    kv_finish()

    key_count = plane_size * rows
    hc = qs.shape[2]

    def plane_keys():
        return kv[0].reshape(key_count, hc), kv[1].reshape(key_count, hc)

    def part_copy(source_plane, target_plane):
        return remote(
            sent_part.at[target_plane],
            got_part.at[source_plane],
            part_send.at[target_plane],
            part_recv.at[source_plane],
            on_line(target_plane),
        )

    def level_copy(source_plane, target_plane):
        return remote(
            sent_level.at[target_plane],
            got_level.at[source_plane],
            level_send.at[target_plane],
            level_recv.at[source_plane],
            on_line(target_plane),
        )

    def later_plane(other):
        query_copy(other, plane).wait_recv()
        keys, values = plane_keys()
        part, levels = attend(qs[other], keys, values, None)
        sent_part[other] = part.astype(jnp.bfloat16)
        sent_level[other] = to_lanes(levels)
        part_copy(plane, other).start()
        level_copy(plane, other).start()

    each(plane + 1, planes, later_plane)
    keys, values = plane_keys()
    part, levels = attend(qs[plane], keys, values, place * rows)
    own_part[...] = part
    own_level[...] = levels

    side_forward()

    def join(other, state):
        mixed, peak, total = state
        part_copy(other, plane).wait_recv()
        level_copy(other, plane).wait_recv()
        level = to_columns(got_level[other], rows)
        new_peak = jnp.maximum(peak, level)
        keep = jnp.exp(peak - new_peak)
        add = jnp.exp(level - new_peak)
        mixed = mixed * spread(keep, hc) + got_part[other].astype(jnp.float32) * spread(add, hc)
        return mixed, new_peak, total * keep + add

    mixed, _, total = lax.fori_loop(
        0, plane, join, (own_part[...], own_level[...], jnp.ones((rows, 128), jnp.float32))
    )
    attn_self = (mixed / spread(total, hc)).astype(jnp.bfloat16)

    def exchange(source, target, send, recv):
        def copy(step):
            other = head_at(step)
            return remote(
                source(other), target(head), send.at[other], recv.at[head], (ctx, other)
            )

        def arrival(step):
            other = head_at(step)
            return remote(
                source(other), target(other), send.at[other], recv.at[other], (ctx, other)
            )

        def start():
            each(1, head_devices, lambda step: copy(step).start())

        def finish():
            each(1, head_devices, lambda step: arrival(step).wait_recv())

        def drain():
            each(1, head_devices, lambda step: copy(step).wait_send())

        return start, finish, drain

    loads[3].wait()
    terms_start, terms_finish, terms_drain = exchange(
        lambda other: out_terms.at[other], lambda slot: got_terms.at[slot], terms_send, terms_recv
    )
    for index in range(head_devices):
        out_terms[index] = matmul(
            attn_self, weights[3, index * share : (index + 1) * share], NT
        ).astype(jnp.bfloat16)
    terms_start()
    terms_finish()
    columns = pl.ds(pl.multiple_of(head * share, share), share)
    mixed_rows = hidden[:, columns].astype(jnp.float32) + out_terms[head].astype(jnp.float32)
    for step in range(1, head_devices):
        mixed_rows = mixed_rows + got_terms[head_at(step)].astype(jnp.float32)

    shares[head] = (mixed_rows * cross_gain[:, columns]).astype(jnp.bfloat16)
    square = jnp.sum(mixed_rows * mixed_rows, axis=1, keepdims=True)
    squares[head] = to_lanes(jnp.broadcast_to(square, (rows, 128)))
    share_start, share_finish, share_drain = exchange(
        lambda other: shares.at[head], lambda slot: shares.at[slot], share_send, share_recv
    )
    square_start, square_finish, square_drain = exchange(
        lambda other: squares.at[head], lambda slot: squares.at[slot], square_send, square_recv
    )
    square_start()
    share_start()

    side_finish()
    side_rows = planes * plane_size * side.shape[3]

    square_finish()
    share_finish()
    all_squares = squares[0]
    for index in range(1, head_devices):
        all_squares = all_squares + squares[index]
    scale = lax.rsqrt(to_columns(all_squares, rows)[:, :1] / width + epsilon)
    query_weights = side[2].reshape(side_rows, hc)
    cross_q = jnp.zeros((rows, hc), jnp.float32)
    for index in range(head_devices):
        cross_q = cross_q + matmul(
            shares[index], query_weights[index * share : (index + 1) * share]
        )
    cross_q = (cross_q * scale).astype(jnp.bfloat16)
    attn_cross, _ = attend(
        cross_q, side[0].reshape(side_rows, hc), side[1].reshape(side_rows, hc), None
    )
    attn_cross = attn_cross.astype(jnp.bfloat16)
    out_weights = side[3].reshape(side_rows, hc)
    for index in range(head_devices):
        final_terms[index] = matmul(
            attn_cross, out_weights[index * share : (index + 1) * share], NT
        ).astype(jnp.bfloat16)
    final_start, final_finish, final_drain = exchange(
        lambda other: final_terms.at[other], lambda slot: got_final.at[slot], final_send, final_recv
    )
    final_start()
    final_finish()
    result = mixed_rows + final_terms[head].astype(jnp.float32)
    for step in range(1, head_devices):
        result = result + got_final[head_at(step)].astype(jnp.float32)
    out[...] = result.astype(jnp.bfloat16)

    each(1, planes, lambda step: side_line(step, plane).wait_send())
    kv_drain()
    side_drain()
    each(0, plane, lambda target: query_copy(plane, target).wait_send())
    each(plane + 1, planes, lambda other: part_copy(plane, other).wait_send())
    each(plane + 1, planes, lambda other: level_copy(plane, other).wait_send())
    terms_drain()
    share_drain()
    square_drain()
    final_drain()


def body(
    plane_size,
    hidden,
    self_gain,
    cross_gain,
    self_query,
    self_key,
    self_value,
    self_out,
    cross_query,
    cross_out,
    enc_key,
    enc_value,
):
    rows, width = hidden.shape
    hc = self_query.shape[1]
    ctx_devices = lax.axis_size("ctx")
    head_devices = lax.axis_size("head")
    planes = ctx_devices // plane_size
    chips = plane_size // CORES
    share = width // head_devices
    piece = enc_key.shape[0]
    low, full = jnp.bfloat16, jnp.float32
    vmem = pl.BlockSpec(memory_space=pltpu.VMEM)
    hbm = pl.BlockSpec(memory_space=pl.ANY)
    dma = pltpu.SemaphoreType.DMA
    return pl.pallas_call(
        functools.partial(kernel, planes, plane_size, head_devices),
        out_shape=jax.ShapeDtypeStruct((rows, share), low),
        in_specs=[vmem] * 3 + [hbm] * 4 + [vmem] * 4,
        out_specs=vmem,
        scratch_shapes=[
            pltpu.VMEM((4, width, hc), low),
            pltpu.VMEM((rows, width), low),
            pltpu.VMEM((2, plane_size, rows, hc), low),
            pltpu.VMEM((planes, rows, hc), low),
            pltpu.VMEM((planes, rows, hc), low),
            pltpu.VMEM((planes, 8, 128), full),
            pltpu.VMEM((planes, rows, hc), low),
            pltpu.VMEM((planes, 8, 128), full),
            pltpu.VMEM((rows, hc), full),
            pltpu.VMEM((rows, 128), full),
            pltpu.VMEM((4, planes, plane_size, piece, hc), low),
            pltpu.VMEM((head_devices, rows, share), low),
            pltpu.VMEM((head_devices, rows, share), low),
            pltpu.VMEM((head_devices, rows, share), low),
            pltpu.VMEM((head_devices, 8, 128), full),
            pltpu.VMEM((head_devices, rows, share), low),
            pltpu.VMEM((head_devices, rows, share), low),
            dma((4,)),
            dma((2 * chips,)),
            dma((plane_size,)),
            dma((planes,)),
            dma((planes,)),
            dma((2 * chips,)),
            dma((plane_size,)),
        ]
        + [dma((planes,))] * 6
        + [dma((head_devices,))] * 8,
        compiler_params=pltpu.CompilerParams(
            collective_id=0, has_side_effects=True, vmem_limit_bytes=48 * 1024 * 1024
        ),
    )(
        hidden,
        self_gain.reshape(1, width),
        cross_gain.reshape(1, width),
        self_query,
        self_key,
        self_value,
        self_out,
        enc_key,
        enc_value,
        cross_query,
        cross_out,
    )


def solution(mesh, plane_size=PLANE):
    placed = (
        P("ctx", None),
        P(),
        P(),
        P(None, "head"),
        P(None, "head"),
        P(None, "head"),
        P(None, "head"),
        P("ctx", "head"),
        P("ctx", "head"),
        P("ctx", "head"),
        P("ctx", "head"),
    )
    return jax.shard_map(
        functools.partial(body, plane_size),
        mesh=mesh,
        in_specs=placed,
        out_specs=P("ctx", "head"),
        check_vma=False,
    )
```

time: 1410 us -> 91.7 us (0.07)
  waiting for transfers between devices: 1330 us -> 0 us
  Pallas kernels: 0 us -> 80 us
  matrix products: 31.3 us -> 0 us
    all_gather x6 -> x0, waiting for transfers between devices: 1250 us -> none  [the longest x1 220 us: body(): lax.all_gather(key_rows, 'ctx', axis=0, tiled=True)]
    pallas_call x0 -> x1, Pallas kernels: none -> 80 us  [body(): pl.pallas_call(functools.partial(kernel, planes, plane_size, head_devices...]
    psum x1 -> x0, waiting for transfers between devices: 55.6 us -> none  [body(): lax.psum(partial_terms.astype(jnp.bfloat16), 'head').astype(jnp.float32)]
    dot_general x10 -> x0, matrix products: 31.3 us -> none  [the longest x2 10.1 us: fold_piece(): jnp.einsum('qhd,khd->hqk', shaped_queries, key_heads, preferred_element_t...]
    reduce_scatter x1 -> x0, waiting for transfers between devices: 26.4 us -> none  [body(): lax.psum_scatter(out_partial.astype(jnp.bfloat16), 'head', scatter_dimens...]
    all_gather x4 -> x0, local copies, waits for them, and re-layouts: 18.9 us -> none  [the longest x1 7.97 us: body(): lax.all_gather(key_rows, 'ctx', axis=0, tiled=True)]
  transfers between devices with their start and end apart: 8 -> 0, of which waited for: 8 -> 0; matrix products, arithmetic and copies ran while one was open for 4% -> 0% of each run, Pallas kernels for 0% -> 0%
where the time goes in v1:
time: 91.7 us; the launch traced here: 90.7 us
  Pallas kernels  80 us (87%)
  local copies, waits for them, and re-layouts  10.7 us (12%)
    pallas_call x1, Pallas kernels, body(): pl.pallas_call(functools.partial(kernel, planes, plane_size, head_devices...  80 us
    unnamed x23, local copies, waits for them, and re-layouts  10.7 us

profile of v1, /device:TPU:1, one launch (start us, length us, event | category | flops | bytes accessed | tf_op | source)
XLA Modules:
  0.0 90.7 jit_solution(6531996423725950733)
XLA Ops:
  0.0 0.0 copy-start
  0.0 1.2 %copy-done = bf16[2048,256]{1,0:T(8,128)(2,1)S(1)} copy-done((bf16[2048,256]{1,0:T(8,128)(2,1)S(1)}, bf16[2048,256]{1,0:T(8,128)(2,1)}, u32[]{:S(2)}) %copy-start) | copy-done | bytes 1048600
  1.2 0.0 copy-start.1
  1.2 1.2 %copy-done.1 = bf16[2048,256]{1,0:T(8,128)(2,1)S(1)} copy-done((bf16[2048,256]{1,0:T(8,128)(2,1)S(1)}, bf16[2048,256]{1,0:T(8,128)(2,1)}, u32[]{:S(2)}) %copy-start.1) | copy-done | bytes 1048600
  2.5 0.0 copy-start.2
  2.5 1.2 %copy-done.2 = bf16[2048,256]{1,0:T(8,128)(2,1)S(1)} copy-done((bf16[2048,256]{1,0:T(8,128)(2,1)S(1)}, bf16[2048,256]{1,0:T(8,128)(2,1)}, u32[]{:S(2)}) %copy-start.2) | copy-done | bytes 1048600
  3.7 0.0 copy-start.3
  3.7 1.2 %copy-done.3 = bf16[2048,256]{1,0:T(8,128)(2,1)S(1)} copy-done((bf16[2048,256]{1,0:T(8,128)(2,1)S(1)}, bf16[2048,256]{1,0:T(8,128)(2,1)}, u32[]{:S(2)}) %copy-start.3) | copy-done | bytes 1048600
  4.9 0.0 copy-start.4
  4.9 1.0 %copy-done.4 = bf16[80,2048]{1,0:T(8,128)(2,1)S(1)} copy-done((bf16[80,2048]{1,0:T(8,128)(2,1)S(1)}, bf16[80,2048]{1,0:T(8,128)(2,1)}, u32[]{:S(2)}) %copy-start.4) | copy-done | bytes 327704
  5.9 0.0 copy-start.5
  5.9 0.7 copy-done.5
  6.6 0.0 copy-start.6
  6.6 0.7 copy-done.6
  7.3 0.0 copy-start.7
  7.3 0.7 copy-done.7
  8.0 0.0 copy-start.8
  8.0 0.7 copy-done.8
  8.7 0.0 copy-start.9
  8.7 0.7 copy-done.9
  9.4 0.0 copy-start.10
  9.4 0.7 copy-done.10
  10.1 80.0 %shard_map.109 = bf16[80,512]{1,0:T(8,128)(2,1)S(1)} custom-call(bf16[80,2048]{1,0:T(8,128)(2,1)S(1)} %copy-done.4, f32[1,2048]{1,0:T(1,128)S(1)} %bitcast.2, f32[1,2048]{1,0:T(1,128)S(1)} %bitcast.3, bf16[2048,256]{1,0:T(8,128)(2,1)S(1)} %copy-done, bf16[2048,256]{1,0:T(8,128)(2,1)S(1)} %copy-done.1, bf16[2048,256]{1,0:T(8,128)(2,1)S(1)} %copy-done.2, ...), custom_call_target="tpu_custom_call" | custom-call | tf_op jit(solution)/shard_map/pallas_call | solution.py:455
  90.1 0.6 copy.13
Async XLA Ops:
  0.0 1.2 %copy-start = (bf16[2048,256]{1,0:T(8,128)(2,1)S(1)}, bf16[2048,256]{1,0:T(8,128)(2,1)}, u32[]{:S(2)}) copy-start(bf16[2048,256]{1,0:T(8,128)(2,1)} %self_query.1) | copy-start | bytes 3145732
  1.2 1.2 %copy-start.1 = (bf16[2048,256]{1,0:T(8,128)(2,1)S(1)}, bf16[2048,256]{1,0:T(8,128)(2,1)}, u32[]{:S(2)}) copy-start(bf16[2048,256]{1,0:T(8,128)(2,1)} %self_key.1) | copy-start | bytes 3145732
  2.5 1.2 %copy-start.2 = (bf16[2048,256]{1,0:T(8,128)(2,1)S(1)}, bf16[2048,256]{1,0:T(8,128)(2,1)}, u32[]{:S(2)}) copy-start(bf16[2048,256]{1,0:T(8,128)(2,1)} %self_value.1) | copy-start | bytes 3145732
  3.7 1.2 %copy-start.3 = (bf16[2048,256]{1,0:T(8,128)(2,1)S(1)}, bf16[2048,256]{1,0:T(8,128)(2,1)}, u32[]{:S(2)}) copy-start(bf16[2048,256]{1,0:T(8,128)(2,1)} %self_out.1) | copy-start | bytes 3145732
  4.9 1.0 %copy-start.4 = (bf16[80,2048]{1,0:T(8,128)(2,1)S(1)}, bf16[80,2048]{1,0:T(8,128)(2,1)}, u32[]{:S(2)}) copy-start(bf16[80,2048]{1,0:T(8,128)(2,1)} %hidden.1) | copy-start | bytes 983044
  5.9 0.7 copy-start.5
  6.6 0.7 copy-start.6
  7.3 0.7 copy-start.7
  8.0 0.7 copy-start.8
  8.7 0.7 copy-start.9
  9.4 0.7 copy-start.10

commit v2 on v1

v2 whole, which is shorter than its diff:
```python
import functools

import jax
import jax.numpy as jnp
from jax import lax
from jax.experimental import pallas as pl
from jax.experimental.pallas import tpu as pltpu
from jax.sharding import PartitionSpec as P

KV = 64
PLANE = 16
VMEM_BYTES = 62 * 1024 * 1024
MESH = pl.DeviceIdType.MESH

epsilon = 1e-06

NT = (((1,), (1,)), ((), ()))
NN = (((1,), (0,)), ((), ()))


def matmul(left, right, dims=NN):
    return lax.dot_general(left, right, dims, preferred_element_type=jnp.float32)


def to_lanes(columns):
    rows = columns.shape[0]
    square = jnp.concatenate([columns, jnp.zeros((128 - rows, 128), jnp.float32)], axis=0)
    return jnp.transpose(square)[:8]


def to_columns(lanes, rows):
    square = jnp.concatenate([lanes, jnp.zeros((120, 128), jnp.float32)], axis=0)
    return jnp.transpose(square)[:rows]


def spread(per_head, width):
    rows = per_head.shape[0]
    owner = lax.broadcasted_iota(jnp.int32, (rows, width), 1) // KV
    result = jnp.zeros((rows, width), jnp.float32)
    for head in range(width // KV):
        result = jnp.where(owner == head, per_head[:, head : head + 1], result)
    return result


def attend(queries, keys, values, first_query):
    rows, width = queries.shape
    heads = width // KV
    owner = lax.broadcasted_iota(jnp.int32, (rows, width), 1) // KV
    zero = jnp.zeros_like(queries)
    stacked = jnp.concatenate(
        [jnp.where(owner == head, queries, zero) for head in range(heads)], axis=0
    )
    scores = matmul(stacked, keys, NT)
    if first_query is not None:
        token = lax.broadcasted_iota(jnp.int32, (rows, scores.shape[1]), 0) + first_query
        seen = lax.broadcasted_iota(jnp.int32, (rows, scores.shape[1]), 1) <= token
        scores = jnp.where(
            jnp.concatenate([seen] * heads, axis=0), scores, jnp.float32(-1e30)
        )
    peak = jnp.max(scores, axis=1, keepdims=True)
    weights = jnp.exp(scores - peak)
    total = jnp.sum(weights, axis=1, keepdims=True)
    mixed = matmul(weights.astype(jnp.bfloat16), values)
    mixed = mixed / total
    level = peak + jnp.log(total)
    result = jnp.zeros((rows, width), jnp.float32)
    levels = jnp.zeros((rows, 128), jnp.float32)
    column = lax.broadcasted_iota(jnp.int32, (rows, 128), 1)
    for head in range(heads):
        part = slice(head * rows, (head + 1) * rows)
        result = jnp.where(owner == head, mixed[part], result)
        levels = jnp.where(column == head, level[part], levels)
    return result, levels


def place_gather(buffer, send, recv, position, sizes, device_of):
    x, l, core = position
    x_size, device_count = sizes
    own = x * 4 + l * 2 + core
    across = x * 4 + (1 - l) * 2 + core
    sibling = device_of(x * 4 + l * 2 + 1 - core)
    partner = device_of(across)

    def slot_at(step, pair):
        return lax.rem(x + step, x_size) * 4 + pair * 2 + core

    def copy(slot, sender, device):
        return pltpu.make_async_remote_copy(
            src_ref=buffer(slot),
            dst_ref=buffer(slot),
            send_sem=send.at[sender],
            recv_sem=recv.at[slot],
            device_id=device,
            device_id_type=MESH,
        )

    def arrived(slot):
        copy(slot, 0, sibling).wait_recv()

    def to_sibling(slot, sender):
        copy(slot, sender, sibling).start()

    def to_partner(slot, sender):
        copy(slot, sender, partner).start()

    def to_line(slot, sender):
        each(1, x_size, lambda step: copy(slot, sender + step, device_of(slot_at(step, l))).start())

    def finish():
        each(0, device_count // 2, lambda step: arrived(step * 2 + 1 - core))

    class Pair:
        @staticmethod
        def start():
            to_partner(own, 0)
            to_sibling(own, 1)

        @staticmethod
        def start_line():
            to_line(own, 1)

        @staticmethod
        def middle():
            arrived(across)
            to_line(across, x_size)
            to_sibling(across, 2 * x_size)

        @staticmethod
        def forward():
            def one(step):
                arrived(slot_at(step, l))
                to_sibling(slot_at(step, l), 2 * x_size + step)

            each(1, x_size, one)

        @staticmethod
        def forward_across():
            def one(step):
                arrived(slot_at(step, 1 - l))
                to_sibling(slot_at(step, 1 - l), 3 * x_size - 1 + step)

            each(1, x_size, one)

    class Line:
        @staticmethod
        def start():
            to_line(own, -1)
            to_partner(own, x_size - 1)
            to_sibling(own, x_size)

        @staticmethod
        def forward():
            def one(step):
                arrived(slot_at(step, l))
                to_partner(slot_at(step, l), x_size + step)
                to_sibling(slot_at(step, l), 2 * x_size - 1 + step)

            each(1, x_size, one)

        @staticmethod
        def forward_across():
            def one(step):
                arrived(slot_at(step, 1 - l))
                to_sibling(slot_at(step, 1 - l), 3 * x_size - 1 + step)

            each(0, x_size, one)

    def drain():
        each(0, 4 * x_size - 1, lambda sender: copy(own, sender, sibling).wait_send())

    Pair.finish = Line.finish = staticmethod(finish)
    Pair.drain = Line.drain = staticmethod(drain)
    return Pair, Line


def each(low, high, step_fn):
    def step(index, carry):
        step_fn(index)
        return carry

    lax.fori_loop(low, high, step, 0)


def kernel(
    planes,
    plane_size,
    head_devices,
    hidden_in,
    self_gain_in,
    cross_gain_in,
    self_query,
    self_key,
    self_value,
    self_out,
    enc_key,
    enc_value,
    cross_query,
    cross_out,
    out,
    hidden,
    self_gain,
    cross_gain,
    weights,
    normed,
    kv,
    qs,
    sent_part,
    sent_level,
    got_part,
    got_level,
    own_part,
    own_level,
    side,
    out_weights,
    last_own,
    last_weights,
    mixed_rows,
    attn_self,
    attn_cross,
    load_sem,
    kv_send,
    kv_recv,
    side_send,
    side_recv,
    so_send,
    so_recv,
    last_send,
    last_recv,
    side_z_send,
    side_z_recv,
    q_send,
    q_recv,
    part_send,
    part_recv,
    level_send,
    level_recv,
    last_z_send,
    last_z_recv,
    so_y_send,
    so_y_recv,
    last_y_send,
    last_y_recv,
    self_send,
    self_recv,
    cross_send,
    cross_recv,
):
    rows, width = hidden.shape
    share = width // head_devices
    x_size = plane_size // 4
    ctx = lax.axis_index("ctx")
    head = lax.axis_index("head")
    plane = ctx // plane_size
    place = ctx % plane_size
    position = (place // 4, (place // 2) % 2, place % 2)
    per_head = planes // head_devices
    last_head = plane // per_head
    last_slot = plane % per_head

    def in_plane(other_place):
        return (plane * plane_size + other_place, head)

    def on_line(other_plane):
        return (other_plane * plane_size + place, head)

    def line_plane(step):
        return (plane + step) % planes

    def head_at(step):
        return (head + step) % head_devices

    def remote(src, dst, send, recv, device):
        return pltpu.make_async_remote_copy(
            src_ref=src,
            dst_ref=dst,
            send_sem=send,
            recv_sem=recv,
            device_id=device,
            device_id_type=MESH,
        )

    barrier = pltpu.get_barrier_semaphore()

    def greet(device):
        pl.semaphore_signal(barrier, inc=1, device_id=device, device_id_type=MESH)

    x, l, core = position

    def line_place(step):
        return lax.rem(x + step, x_size) * 4 + l * 2 + core

    each(1, x_size, lambda step: greet(in_plane(line_place(step))))
    greet(in_plane(x * 4 + (1 - l) * 2 + core))
    greet(in_plane(x * 4 + l * 2 + 1 - core))
    each(1, planes, lambda step: greet(on_line(line_plane(step))))
    each(1, head_devices, lambda step: greet((ctx, head_at(step))))

    loads = [
        pltpu.make_async_copy(source, target, load_sem.at[index])
        for index, (source, target) in enumerate(
            (
                (hidden_in, hidden),
                (self_gain_in, self_gain),
                (self_key, weights.at[0]),
                (self_value, weights.at[1]),
                (self_query, weights.at[2]),
                (self_out, out_weights.at[0]),
                (enc_key, side.at[0, plane, place]),
                (enc_value, side.at[1, plane, place]),
                (cross_query, side.at[2, plane, place]),
                (cross_out, last_own),
                (cross_gain_in, cross_gain),
            )
        )
    ]
    for load in loads:
        load.start()

    loads[0].wait()
    loads[1].wait()
    inputs = hidden[...].astype(jnp.float32)
    mean_square = jnp.mean(inputs * inputs, axis=1, keepdims=True)
    normed[...] = (inputs * lax.rsqrt(mean_square + epsilon) * self_gain[...]).astype(jnp.bfloat16)
    for index in range(2):
        loads[2 + index].wait()
        kv[index, place] = matmul(normed[...], weights[index]).astype(jnp.bfloat16)
    loads[4].wait()
    qs[plane] = matmul(normed[...], weights[2]).astype(jnp.bfloat16)
    for load in loads[5:]:
        load.wait()

    pl.semaphore_wait(barrier, (x_size - 1) + 2 + (planes - 1) + (head_devices - 1))

    sizes = (x_size, plane_size)
    kv_pair, _ = place_gather(
        lambda slot: kv.at[:, slot], kv_send, kv_recv, position, sizes, in_plane
    )
    side_pair, _ = place_gather(
        lambda slot: side.at[:, :, slot], side_send, side_recv, position, sizes, in_plane
    )
    _, so_line = place_gather(
        lambda slot: out_weights.at[pl.ds(1, head_devices - 1), slot],
        so_send,
        so_recv,
        position,
        sizes,
        in_plane,
    )
    last_pair, _ = place_gather(
        lambda slot: last_weights.at[:, :, slot], last_send, last_recv, position, sizes, in_plane
    )

    def query_copy(source_plane, target_plane):
        return remote(
            qs.at[source_plane],
            qs.at[source_plane],
            q_send.at[target_plane],
            q_recv.at[source_plane],
            on_line(target_plane),
        )

    def side_line(step, other):
        block = side.at[:, other, place]
        return remote(
            block, block, side_z_send.at[step], side_z_recv.at[other], on_line(line_plane(step))
        )

    def so_heads(step):
        other = head_at(step)
        return remote(
            out_weights.at[0, place],
            out_weights.at[head_devices - step, place],
            so_y_send.at[step],
            so_y_recv.at[head_devices - step],
            (ctx, other),
        )

    def last_heads(source, target):
        return remote(
            last_own,
            last_weights.at[last_slot, source, place],
            last_y_send.at[0],
            last_y_recv.at[source],
            (ctx, target),
        )

    def last_line(step, slot):
        block = last_weights.at[slot, :, place]
        return remote(
            block, block, last_z_send.at[step], last_z_recv.at[slot], on_line(line_plane(step))
        )

    kv_pair.start()
    kv_pair.start_line()
    each(0, plane, lambda target: query_copy(plane, target).start())
    each(1, head_devices, lambda step: so_heads(step).start())

    @pl.when(head != last_head)
    def _():
        last_heads(head, last_head).start()

    each(1, planes, lambda step: side_line(step, plane).start())
    kv_pair.middle()
    kv_pair.forward()
    kv_pair.forward_across()
    kv_pair.finish()

    each(1, head_devices, lambda step: so_heads(step).wait_recv())
    so_line.start()

    @pl.when(head == last_head)
    def _():
        last_weights[last_slot, head, place] = last_own[...]
        each(1, head_devices, lambda step: last_heads(head_at(step), head).wait_recv())
        each(1, planes, lambda step: last_line(step, last_slot).start())

    each(1, planes, lambda step: side_line(step, line_plane(step)).wait_recv())
    side_pair.start()
    side_pair.start_line()

    key_count = plane_size * rows
    hc = qs.shape[2]

    def part_copy(source_plane, target_plane):
        return remote(
            sent_part.at[target_plane],
            got_part.at[source_plane],
            part_send.at[target_plane],
            part_recv.at[source_plane],
            on_line(target_plane),
        )

    def level_copy(source_plane, target_plane):
        return remote(
            sent_level.at[target_plane],
            got_level.at[source_plane],
            level_send.at[target_plane],
            level_recv.at[source_plane],
            on_line(target_plane),
        )

    each(plane + 1, planes, lambda other: query_copy(other, plane).wait_recv())

    def later_planes(low, high):
        for step in reversed(range(low, high)):
            other = line_plane(step)
            part, levels = attend(
                qs[other], kv[0].reshape(key_count, hc), kv[1].reshape(key_count, hc), None
            )
            sent_part[other] = part.astype(jnp.bfloat16)
            sent_level[other] = to_lanes(levels)

        def send(step):
            part_copy(plane, plane + step).start()
            level_copy(plane, plane + step).start()

        each(low, jnp.minimum(high, planes - plane), send)

    half = planes // 2

    if half > 1:

        @pl.when(plane < half)
        def _():
            later_planes(half, planes)

    part, levels = attend(
        qs[plane], kv[0].reshape(key_count, hc), kv[1].reshape(key_count, hc), place * rows
    )
    own_part[...] = part
    own_level[...] = levels
    later_planes(1, half if half > 1 else planes)

    so_line.forward()
    side_pair.middle()

    def join(other, state):
        mixed, peak, total = state
        part_copy(other, plane).wait_recv()
        level_copy(other, plane).wait_recv()
        level = to_columns(got_level[other], rows)
        new_peak = jnp.maximum(peak, level)
        keep = jnp.exp(peak - new_peak)
        add = jnp.exp(level - new_peak)
        mixed = mixed * spread(keep, hc) + got_part[other].astype(jnp.float32) * spread(add, hc)
        return mixed, new_peak, total * keep + add

    mixed, _, total = lax.fori_loop(
        0, plane, join, (own_part[...], own_level[...], jnp.ones((rows, 128), jnp.float32))
    )
    attn_self[head] = (mixed / spread(total, hc)).astype(jnp.bfloat16)

    def exchange(buffer, send, recv):
        def copy(slot, step):
            return remote(
                buffer.at[slot],
                buffer.at[slot],
                send.at[step],
                recv.at[slot],
                (ctx, head_at(step)),
            )

        def start():
            each(1, head_devices, lambda step: copy(head, step).start())

        def finish(step):
            copy(head_at(step), step).wait_recv()

        def drain():
            each(1, head_devices, lambda step: copy(head, step).wait_send())

        return start, finish, drain

    self_start, self_finish, self_drain = exchange(attn_self, self_send, self_recv)
    self_start()
    so_line.forward_across()
    side_pair.forward()
    so_line.finish()

    def self_term(step):
        return matmul(attn_self[head_at(step)], out_weights[step].reshape(width, hc), NT)

    mixed_rows[...] = hidden[...].astype(jnp.float32) + self_term(0)
    for step in range(1, head_devices):
        self_finish(step)
        mixed_rows[...] += self_term(step)
    whole_rows = mixed_rows[...]
    mean_square = jnp.mean(whole_rows * whole_rows, axis=1, keepdims=True)
    normed[...] = (
        whole_rows * lax.rsqrt(mean_square + epsilon) * cross_gain[...]
    ).astype(jnp.bfloat16)

    def last_arrival(slot):
        @pl.when(plane != head * per_head + slot)
        def _():
            last_line(1, slot).wait_recv()

    each(0, per_head, last_arrival)
    last_pair.start()
    last_pair.start_line()
    side_pair.forward_across()
    side_pair.finish()

    side_rows = planes * plane_size * side.shape[3]
    cross_q = matmul(normed[...], side[2].reshape(side_rows, hc)).astype(jnp.bfloat16)
    crossed, _ = attend(
        cross_q, side[0].reshape(side_rows, hc), side[1].reshape(side_rows, hc), None
    )
    attn_cross[head] = crossed.astype(jnp.bfloat16)
    cross_start, cross_finish, cross_drain = exchange(attn_cross, cross_send, cross_recv)
    cross_start()
    last_pair.middle()
    last_pair.forward()
    last_pair.forward_across()
    last_pair.finish()

    columns = pl.ds(pl.multiple_of(head * share, share), share)
    result = mixed_rows[:, columns]
    for step in range(head_devices):
        if step:
            cross_finish(step)
        other = head_at(step)
        terms = [
            matmul(
                attn_cross[other],
                last_weights[slot, other].reshape(share // per_head, hc),
                NT,
            )
            for slot in range(per_head)
        ]
        result = result + jnp.concatenate(terms, axis=1)
    out[...] = result.astype(jnp.bfloat16)

    each(1, planes, lambda step: side_line(step, plane).wait_send())
    each(1, head_devices, lambda step: so_heads(step).wait_send())

    @pl.when(head != last_head)
    def _():
        last_heads(head, last_head).wait_send()

    @pl.when(head == last_head)
    def _():
        each(1, planes, lambda step: last_line(step, last_slot).wait_send())

    kv_pair.drain()
    side_pair.drain()
    so_line.drain()
    last_pair.drain()
    each(0, plane, lambda target: query_copy(plane, target).wait_send())
    each(plane + 1, planes, lambda other: part_copy(plane, other).wait_send())
    each(plane + 1, planes, lambda other: level_copy(plane, other).wait_send())
    self_drain()
    cross_drain()


def body(
    plane_size,
    hidden,
    self_gain,
    cross_gain,
    self_query,
    self_key,
    self_value,
    self_out,
    cross_query,
    cross_out,
    enc_key,
    enc_value,
):
    rows, width = hidden.shape
    hc = self_query.shape[1]
    ctx_devices = lax.axis_size("ctx")
    head_devices = lax.axis_size("head")
    planes = ctx_devices // plane_size
    share = width // head_devices
    piece = enc_key.shape[0]
    low, full = jnp.bfloat16, jnp.float32
    vmem = pl.BlockSpec(memory_space=pltpu.VMEM)
    hbm = pl.BlockSpec(memory_space=pl.ANY)
    dma = pltpu.SemaphoreType.DMA
    return pl.pallas_call(
        functools.partial(kernel, planes, plane_size, head_devices),
        out_shape=jax.ShapeDtypeStruct((rows, share), low),
        in_specs=[hbm] * 11,
        out_specs=vmem,
        scratch_shapes=[
            pltpu.VMEM((rows, width), low),
            pltpu.VMEM((1, width), full),
            pltpu.VMEM((1, width), full),
            pltpu.VMEM((3, width, hc), low),
            pltpu.VMEM((rows, width), low),
            pltpu.VMEM((2, plane_size, rows, hc), low),
            pltpu.VMEM((planes, rows, hc), low),
            pltpu.VMEM((planes, rows, hc), low),
            pltpu.VMEM((planes, 8, 128), full),
            pltpu.VMEM((planes, rows, hc), low),
            pltpu.VMEM((planes, 8, 128), full),
            pltpu.VMEM((rows, hc), full),
            pltpu.VMEM((rows, 128), full),
            pltpu.VMEM((3, planes, plane_size, piece, hc), low),
            pltpu.VMEM((head_devices, plane_size, width // plane_size, hc), low),
            pltpu.VMEM((piece, hc), low),
            pltpu.VMEM((planes // head_devices, head_devices, plane_size, piece, hc), low),
            pltpu.VMEM((rows, width), full),
            pltpu.VMEM((head_devices, rows, hc), low),
            pltpu.VMEM((head_devices, rows, hc), low),
            dma((11,)),
        ]
        + [dma((plane_size,))] * 8
        + [dma((planes,))] * 10
        + [dma((head_devices,))] * 8,
        compiler_params=pltpu.CompilerParams(
            collective_id=0, has_side_effects=True, vmem_limit_bytes=VMEM_BYTES
        ),
    )(
        hidden,
        self_gain.reshape(1, width),
        cross_gain.reshape(1, width),
        self_query,
        self_key,
        self_value,
        self_out.reshape(plane_size, width // plane_size, hc),
        enc_key,
        enc_value,
        cross_query,
        cross_out,
    )


def solution(mesh, plane_size=PLANE):
    placed = (
        P("ctx", None),
        P(),
        P(),
        P(None, "head"),
        P(None, "head"),
        P(None, "head"),
        P(None, "head"),
        P("ctx", "head"),
        P("ctx", "head"),
        P("ctx", "head"),
        P("ctx", "head"),
    )
    return jax.shard_map(
        functools.partial(body, plane_size),
        mesh=mesh,
        in_specs=placed,
        out_specs=P("ctx", "head"),
        check_vma=False,
    )
```

time: 91.7 us -> 74.5 us (0.81)
  local copies, waits for them, and re-layouts: 10.7 us -> 1.53 us
  Pallas kernels: 80 us -> 72.8 us
    unnamed x23 -> x1, local copies, waits for them, and re-layouts: 10.7 us -> 1.53 us
    pallas_call x1, Pallas kernels: 80 us -> 72.8 us  [body(): pl.pallas_call(functools.partial(kernel, planes, plane_size, head_devices...]
where the time goes in v2:
time: 74.5 us; the launch traced here: 74.3 us
  Pallas kernels  72.8 us (98%)
  local copies, waits for them, and re-layouts  1.53 us (2%)
    pallas_call x1, Pallas kernels, body(): pl.pallas_call(functools.partial(kernel, planes, plane_size, head_devices...  72.8 us
    unnamed x1, local copies, waits for them, and re-layouts  1.53 us

profile of v2, /device:TPU:1, one launch (start us, length us, event | category | flops | bytes accessed | tf_op | source)
XLA Modules:
  0.0 74.3 jit_solution(353909938106311359)
XLA Ops:
  0.0 72.8 %shard_map.109 = bf16[80,512]{1,0:T(8,128)(2,1)} custom-call(bf16[80,2048]{1,0:T(8,128)(2,1)} %hidden_in.1, f32[1,2048]{1,0:T(1,128)} %bitcast.4, f32[1,2048]{1,0:T(1,128)} %bitcast.5, bf16[2048,256]{1,0:T(8,128)(2,1)} %self_query.1, bf16[2048,256]{1,0:T(8,128)(2,1)} %self_key.1, bf16[2048,256]{1,0:T(8,128)(2,1)} %self_value.1, ...), custom_call_target="tpu_custom_call" | custom-call | tf_op jit(solution)/shard_map/pallas_call | solution.py:621
  72.8 1.5 %copy.13 = bf16[80,512]{1,0:T(8,128)(2,1)} copy(bf16[80,512]{1,0:T(8,128)(2,1)} %shard_map.109) | data formatting | bytes 163840

commit v3 on v2

--- a/solution.py
+++ b/solution.py
@@ -106,10 +106,7 @@
     def to_line(slot, sender):
         each(1, x_size, lambda step: copy(slot, sender + step, device_of(slot_at(step, l))).start())
 
-    def finish():
-        each(0, device_count // 2, lambda step: arrived(step * 2 + 1 - core))
-
-    class Pair:
+    class Gather:
         @staticmethod
         def start():
             to_partner(own, 0)
@@ -141,36 +138,15 @@
 
             each(1, x_size, one)
 
-    class Line:
         @staticmethod
-        def start():
-            to_line(own, -1)
-            to_partner(own, x_size - 1)
-            to_sibling(own, x_size)
+        def finish():
+            each(0, device_count // 2, lambda step: arrived(step * 2 + 1 - core))
 
         @staticmethod
-        def forward():
-            def one(step):
-                arrived(slot_at(step, l))
-                to_partner(slot_at(step, l), x_size + step)
-                to_sibling(slot_at(step, l), 2 * x_size - 1 + step)
-
-            each(1, x_size, one)
-
-        @staticmethod
-        def forward_across():
-            def one(step):
-                arrived(slot_at(step, 1 - l))
-                to_sibling(slot_at(step, 1 - l), 3 * x_size - 1 + step)
-
-            each(0, x_size, one)
-
-    def drain():
-        each(0, 4 * x_size - 1, lambda sender: copy(own, sender, sibling).wait_send())
-
-    Pair.finish = Line.finish = staticmethod(finish)
-    Pair.drain = Line.drain = staticmethod(drain)
-    return Pair, Line
+        def drain():
+            each(0, 4 * x_size - 1, lambda sender: copy(own, sender, sibling).wait_send())
+
+    return Gather
 
 
 def each(low, high, step_fn):
@@ -212,18 +188,24 @@
     own_level,
     side,
     out_weights,
+    query_own,
+    query_weights,
     last_own,
     last_weights,
     mixed_rows,
+    gained,
     attn_self,
     attn_cross,
+    query_terms,
+    got_terms,
+    squares,
     load_sem,
     kv_send,
     kv_recv,
     side_send,
     side_recv,
-    so_send,
-    so_recv,
+    query_send,
+    query_recv,
     last_send,
     last_recv,
     side_z_send,
@@ -234,16 +216,26 @@
     part_recv,
     level_send,
     level_recv,
+    query_z_send,
+    query_z_recv,
     last_z_send,
     last_z_recv,
+    query_y_send,
+    query_y_recv,
+    last_y_send,
+    last_y_recv,
     so_y_send,
     so_y_recv,
-    last_y_send,
-    last_y_recv,
+    so_c_send,
+    so_c_recv,
     self_send,
     self_recv,
     cross_send,
     cross_recv,
+    terms_send,
+    terms_recv,
+    square_send,
+    square_recv,
 ):
     rows, width = hidden.shape
     share = width // head_devices
@@ -254,8 +246,7 @@
     place = ctx % plane_size
     position = (place // 4, (place // 2) % 2, place % 2)
     per_head = planes // head_devices
-    last_head = plane // per_head
-    last_slot = plane % per_head
+    columns = pl.ds(pl.multiple_of(head * share, share), share)
 
     def in_plane(other_place):
         return (plane * plane_size + other_place, head)
@@ -304,16 +295,16 @@
                 (self_key, weights.at[0]),
                 (self_value, weights.at[1]),
                 (self_query, weights.at[2]),
-                (self_out, out_weights.at[0]),
+                (self_out.at[head], out_weights.at[head]),
                 (enc_key, side.at[0, plane, place]),
                 (enc_value, side.at[1, plane, place]),
-                (cross_query, side.at[2, plane, place]),
+                (cross_query, query_own),
                 (cross_out, last_own),
                 (cross_gain_in, cross_gain),
             )
         )
     ]
-    for load in loads:
+    for load in loads[:5]:
         load.start()
 
     loads[0].wait()
@@ -321,32 +312,25 @@
     inputs = hidden[...].astype(jnp.float32)
     mean_square = jnp.mean(inputs * inputs, axis=1, keepdims=True)
     normed[...] = (inputs * lax.rsqrt(mean_square + epsilon) * self_gain[...]).astype(jnp.bfloat16)
+    for load in loads[5:]:
+        load.start()
     for index in range(2):
         loads[2 + index].wait()
         kv[index, place] = matmul(normed[...], weights[index]).astype(jnp.bfloat16)
-    loads[4].wait()
-    qs[plane] = matmul(normed[...], weights[2]).astype(jnp.bfloat16)
-    for load in loads[5:]:
-        load.wait()
 
     pl.semaphore_wait(barrier, (x_size - 1) + 2 + (planes - 1) + (head_devices - 1))
 
     sizes = (x_size, plane_size)
-    kv_pair, _ = place_gather(
+    kv_pair = place_gather(
         lambda slot: kv.at[:, slot], kv_send, kv_recv, position, sizes, in_plane
     )
-    side_pair, _ = place_gather(
+    side_pair = place_gather(
         lambda slot: side.at[:, :, slot], side_send, side_recv, position, sizes, in_plane
     )
-    _, so_line = place_gather(
-        lambda slot: out_weights.at[pl.ds(1, head_devices - 1), slot],
-        so_send,
-        so_recv,
-        position,
-        sizes,
-        in_plane,
-    )
-    last_pair, _ = place_gather(
+    query_pair = place_gather(
+        lambda slot: query_weights.at[:, :, slot], query_send, query_recv, position, sizes, in_plane
+    )
+    last_pair = place_gather(
         lambda slot: last_weights.at[:, :, slot], last_send, last_recv, position, sizes, in_plane
     )
 
@@ -365,54 +349,89 @@
             block, block, side_z_send.at[step], side_z_recv.at[other], on_line(line_plane(step))
         )
 
-    def so_heads(step):
-        other = head_at(step)
+    def so_heads(source, target):
         return remote(
-            out_weights.at[0, place],
-            out_weights.at[head_devices - step, place],
-            so_y_send.at[step],
-            so_y_recv.at[head_devices - step],
-            (ctx, other),
-        )
-
-    def last_heads(source, target):
+            self_out.at[target, core],
+            out_weights.at[source, core],
+            so_y_send.at[target],
+            so_y_recv.at[source],
+            (ctx, target),
+        )
+
+    def so_sibling(source, half):
+        block = out_weights.at[source, half]
         return remote(
-            last_own,
-            last_weights.at[last_slot, source, place],
-            last_y_send.at[0],
-            last_y_recv.at[source],
-            (ctx, target),
-        )
-
-    def last_line(step, slot):
-        block = last_weights.at[slot, :, place]
-        return remote(
-            block, block, last_z_send.at[step], last_z_recv.at[slot], on_line(line_plane(step))
-        )
+            block, block, so_c_send.at[source], so_c_recv.at[source], in_plane(x * 4 + l * 2 + 1 - core)
+        )
+
+    def by_features(buffer, own, y_send, y_recv, z_send, z_recv):
+        target = plane // per_head
+        slot = plane % per_head
+
+        def to_head(source, other):
+            return remote(
+                own, buffer.at[slot, source, place], y_send.at[0], y_recv.at[source], (ctx, other)
+            )
+
+        def line(step, which):
+            block = buffer.at[which, :, place]
+            return remote(block, block, z_send.at[step], z_recv.at[which], on_line(line_plane(step)))
+
+        def start():
+            @pl.when(head != target)
+            def _():
+                to_head(head, target).start()
+
+        def start_line():
+            @pl.when(head == target)
+            def _():
+                buffer[slot, head, place] = own[...]
+                each(1, head_devices, lambda step: to_head(head_at(step), head).wait_recv())
+                each(1, planes, lambda step: line(step, slot).start())
+
+        def finish():
+            def arrival(which):
+                @pl.when(plane != head * per_head + which)
+                def _():
+                    line(1, which).wait_recv()
+
+            each(0, per_head, arrival)
+
+        def drain():
+            @pl.when(head != target)
+            def _():
+                to_head(head, target).wait_send()
+
+            @pl.when(head == target)
+            def _():
+                each(1, planes, lambda step: line(step, slot).wait_send())
+
+        return start, start_line, finish, drain
+
+    query_start, query_line, query_finish, query_drain = by_features(
+        query_weights, query_own, query_y_send, query_y_recv, query_z_send, query_z_recv
+    )
+    last_start, last_line, last_finish, last_drain = by_features(
+        last_weights, last_own, last_y_send, last_y_recv, last_z_send, last_z_recv
+    )
 
     kv_pair.start()
     kv_pair.start_line()
+    loads[4].wait()
+    qs[plane] = matmul(normed[...], weights[2]).astype(jnp.bfloat16)
     each(0, plane, lambda target: query_copy(plane, target).start())
-    each(1, head_devices, lambda step: so_heads(step).start())
-
-    @pl.when(head != last_head)
-    def _():
-        last_heads(head, last_head).start()
-
+    for load in loads[5:]:
+        load.wait()
+    query_start()
+    last_start()
+    each(1, head_devices, lambda step: so_heads(head, head_at(step)).start())
     each(1, planes, lambda step: side_line(step, plane).start())
     kv_pair.middle()
+    query_line()
+    last_line()
     kv_pair.forward()
     kv_pair.forward_across()
     kv_pair.finish()
-
-    each(1, head_devices, lambda step: so_heads(step).wait_recv())
-    so_line.start()
-
-    @pl.when(head == last_head)
-    def _():
-        last_weights[last_slot, head, place] = last_own[...]
-        each(1, head_devices, lambda step: last_heads(head_at(step), head).wait_recv())
-        each(1, planes, lambda step: last_line(step, last_slot).start())
 
     each(1, planes, lambda step: side_line(step, line_plane(step)).wait_recv())
     side_pair.start()
@@ -464,15 +483,29 @@
         def _():
             later_planes(half, planes)
 
+    query_finish()
+    query_pair.start()
+    query_pair.start_line()
+
+    later_planes(1, half if half > 1 else planes)
     part, levels = attend(
         qs[plane], kv[0].reshape(key_count, hc), kv[1].reshape(key_count, hc), place * rows
     )
     own_part[...] = part
     own_level[...] = levels
-    later_planes(1, half if half > 1 else planes)
-
-    so_line.forward()
+
+    query_pair.middle()
     side_pair.middle()
+    last_finish()
+    last_pair.start()
+    last_pair.start_line()
+
+    def so_arrival(step):
+        other = head_at(step)
+        so_heads(other, head).wait_recv()
+        so_sibling(other, core).start()
+
+    each(1, head_devices, so_arrival)
 
     def join(other, state):
         mixed, peak, total = state
@@ -513,49 +546,77 @@
 
     self_start, self_finish, self_drain = exchange(attn_self, self_send, self_recv)
     self_start()
-    so_line.forward_across()
+    last_pair.middle()
+    query_pair.forward()
     side_pair.forward()
-    so_line.finish()
+    each(1, head_devices, lambda step: so_sibling(head_at(step), 1 - core).wait_recv())
 
     def self_term(step):
-        return matmul(attn_self[head_at(step)], out_weights[step].reshape(width, hc), NT)
-
-    mixed_rows[...] = hidden[...].astype(jnp.float32) + self_term(0)
+        other = head_at(step)
+        return matmul(attn_self[other], out_weights[other].reshape(share, hc), NT)
+
+    mixed = hidden[:, columns].astype(jnp.float32) + self_term(0)
     for step in range(1, head_devices):
         self_finish(step)
-        mixed_rows[...] += self_term(step)
-    whole_rows = mixed_rows[...]
-    mean_square = jnp.mean(whole_rows * whole_rows, axis=1, keepdims=True)
-    normed[...] = (
-        whole_rows * lax.rsqrt(mean_square + epsilon) * cross_gain[...]
-    ).astype(jnp.bfloat16)
-
-    def last_arrival(slot):
-        @pl.when(plane != head * per_head + slot)
-        def _():
-            last_line(1, slot).wait_recv()
-
-    each(0, per_head, last_arrival)
-    last_pair.start()
-    last_pair.start_line()
+        mixed = mixed + self_term(step)
+    mixed_rows[...] = mixed
+
+    square = jnp.sum(mixed * mixed, axis=1, keepdims=True)
+    squares[head] = to_lanes(jnp.broadcast_to(square, (rows, 128)))
+    square_start, square_finish, square_drain = exchange(squares, square_send, square_recv)
+    square_start()
+    gained[...] = (mixed * cross_gain[:, columns]).astype(jnp.bfloat16)
+    query_pair.forward_across()
+    query_pair.finish()
+    piece_rows = share // per_head
+
+    def query_term(other):
+        return sum(
+            matmul(
+                gained[:, slot * piece_rows : (slot + 1) * piece_rows],
+                query_weights[slot, other].reshape(piece_rows, hc),
+            )
+            for slot in range(per_head)
+        )
+
+    def term_copy(step, slot):
+        other = head_at(step)
+        return remote(
+            query_terms.at[other],
+            got_terms.at[slot],
+            terms_send.at[step],
+            terms_recv.at[slot],
+            (ctx, other),
+        )
+
+    for step in range(1, head_devices):
+        query_terms[head_at(step)] = query_term(head_at(step)).astype(jnp.bfloat16)
+        term_copy(step, head).start()
+    cross_q = query_term(head)
+
     side_pair.forward_across()
+    last_pair.forward()
     side_pair.finish()
+    all_squares = squares[head]
+    for step in range(1, head_devices):
+        square_finish(step)
+        all_squares = all_squares + squares[head_at(step)]
+        term_copy(step, head_at(step)).wait_recv()
+        cross_q = cross_q + got_terms[head_at(step)].astype(jnp.float32)
+    scale = lax.rsqrt(to_columns(all_squares, rows)[:, :1] / width + epsilon)
+    cross_q = (cross_q * scale).astype(jnp.bfloat16)
 
     side_rows = planes * plane_size * side.shape[3]
-    cross_q = matmul(normed[...], side[2].reshape(side_rows, hc)).astype(jnp.bfloat16)
     crossed, _ = attend(
         cross_q, side[0].reshape(side_rows, hc), side[1].reshape(side_rows, hc), None
     )
     attn_cross[head] = crossed.astype(jnp.bfloat16)
     cross_start, cross_finish, cross_drain = exchange(attn_cross, cross_send, cross_recv)
     cross_start()
-    last_pair.middle()
-    last_pair.forward()
     last_pair.forward_across()
     last_pair.finish()
 
-    columns = pl.ds(pl.multiple_of(head * share, share), share)
-    result = mixed_rows[:, columns]
+    result = mixed_rows[...]
     for step in range(head_devices):
         if step:
             cross_finish(step)
@@ -572,25 +633,21 @@
     out[...] = result.astype(jnp.bfloat16)
 
     each(1, planes, lambda step: side_line(step, plane).wait_send())
-    each(1, head_devices, lambda step: so_heads(step).wait_send())
-
-    @pl.when(head != last_head)
-    def _():
-        last_heads(head, last_head).wait_send()
-
-    @pl.when(head == last_head)
-    def _():
-        each(1, planes, lambda step: last_line(step, last_slot).wait_send())
-
+    each(1, head_devices, lambda step: so_heads(head, head_at(step)).wait_send())
+    each(1, head_devices, lambda step: so_sibling(head_at(step), core).wait_send())
+    query_drain()
+    last_drain()
     kv_pair.drain()
     side_pair.drain()
-    so_line.drain()
+    query_pair.drain()
     last_pair.drain()
     each(0, plane, lambda target: query_copy(plane, target).wait_send())
     each(plane + 1, planes, lambda other: part_copy(plane, other).wait_send())
     each(plane + 1, planes, lambda other: level_copy(plane, other).wait_send())
     self_drain()
     cross_drain()
+    square_drain()
+    each(1, head_devices, lambda step: term_copy(step, head).wait_send())
 
 
 def body(
@@ -637,18 +694,24 @@
             pltpu.VMEM((planes, 8, 128), full),
             pltpu.VMEM((rows, hc), full),
             pltpu.VMEM((rows, 128), full),
-            pltpu.VMEM((3, planes, plane_size, piece, hc), low),
-            pltpu.VMEM((head_devices, plane_size, width // plane_size, hc), low),
+            pltpu.VMEM((2, planes, plane_size, piece, hc), low),
+            pltpu.VMEM((head_devices, 2, share // 2, hc), low),
             pltpu.VMEM((piece, hc), low),
             pltpu.VMEM((planes // head_devices, head_devices, plane_size, piece, hc), low),
-            pltpu.VMEM((rows, width), full),
+            pltpu.VMEM((piece, hc), low),
+            pltpu.VMEM((planes // head_devices, head_devices, plane_size, piece, hc), low),
+            pltpu.VMEM((rows, share), full),
+            pltpu.VMEM((rows, share), low),
             pltpu.VMEM((head_devices, rows, hc), low),
             pltpu.VMEM((head_devices, rows, hc), low),
+            pltpu.VMEM((head_devices, rows, hc), low),
+            pltpu.VMEM((head_devices, rows, hc), low),
+            pltpu.VMEM((head_devices, 8, 128), full),
             dma((11,)),
         ]
         + [dma((plane_size,))] * 8
-        + [dma((planes,))] * 10
-        + [dma((head_devices,))] * 8,
+        + [dma((planes,))] * 12
+        + [dma((head_devices,))] * 16,
         compiler_params=pltpu.CompilerParams(
             collective_id=0, has_side_effects=True, vmem_limit_bytes=VMEM_BYTES
         ),
@@ -659,7 +722,7 @@
         self_query,
         self_key,
         self_value,
-        self_out.reshape(plane_size, width // plane_size, hc),
+        self_out.reshape(head_devices, 2, share // 2, hc),
         enc_key,
         enc_value,
         cross_query,

time: 74.5 us -> 66.4 us (0.89); the launches traced: 74.3 us -> 65.3 us
  Pallas kernels: 72.8 us -> 63.8 us
    pallas_call x1, Pallas kernels: 72.8 us -> 63.8 us  [body(): pl.pallas_call(functools.partial(kernel, planes, plane_size, head_devices...]
where the time goes in v3:
time: 66.4 us; the launch traced here: 65.3 us
  Pallas kernels  63.8 us (96%)
  local copies, waits for them, and re-layouts  1.53 us (2%)
    pallas_call x1, Pallas kernels, body(): pl.pallas_call(functools.partial(kernel, planes, plane_size, head_devices...  63.8 us
    unnamed x1, local copies, waits for them, and re-layouts  1.53 us

profile of v3, /device:TPU:1, one launch (start us, length us, event | category | flops | bytes accessed | tf_op | source)
XLA Modules:
  0.0 65.3 jit_solution(9515688109427472379)
XLA Ops:
  0.0 63.8 %shard_map.109 = bf16[80,512]{1,0:T(8,128)(2,1)} custom-call(bf16[80,2048]{1,0:T(8,128)(2,1)} %hidden_in.1, f32[1,2048]{1,0:T(1,128)} %bitcast.4, f32[1,2048]{1,0:T(1,128)} %bitcast.5, bf16[2048,256]{1,0:T(8,128)(2,1)} %self_query.1, bf16[2048,256]{1,0:T(8,128)(2,1)} %self_key.1, bf16[2048,256]{1,0:T(8,128)(2,1)} %self_value.1, ...), custom_call_target="tpu_custom_call" | custom-call | tf_op jit(solution)/shard_map/pallas_call | solution.py:678
  63.8 1.5 %copy.13 = bf16[80,512]{1,0:T(8,128)(2,1)} copy(bf16[80,512]{1,0:T(8,128)(2,1)} %shard_map.109) | data formatting | bytes 163840

commit v4 on v3

--- a/solution.py
+++ b/solution.py
@@ -417,15 +417,15 @@
 
     kv_pair.start()
     kv_pair.start_line()
-    loads[4].wait()
-    qs[plane] = matmul(normed[...], weights[2]).astype(jnp.bfloat16)
-    each(0, plane, lambda target: query_copy(plane, target).start())
     for load in loads[5:]:
         load.wait()
     query_start()
     last_start()
+    each(1, planes, lambda step: side_line(step, plane).start())
+    loads[4].wait()
+    qs[plane] = matmul(normed[...], weights[2]).astype(jnp.bfloat16)
+    each(0, plane, lambda target: query_copy(plane, target).start())
     each(1, head_devices, lambda step: so_heads(head, head_at(step)).start())
-    each(1, planes, lambda step: side_line(step, plane).start())
     kv_pair.middle()
     query_line()
     last_line()

time: 66.4 us -> 65.8 us (level); the launches traced: 65.3 us -> 65.6 us
  no operation moved by 1% of the time
where the time goes in v4:
time: 65.8 us; the launch traced here: 65.6 us
  Pallas kernels  64.1 us (97%)
  local copies, waits for them, and re-layouts  1.53 us (2%)
    pallas_call x1, Pallas kernels, body(): pl.pallas_call(functools.partial(kernel, planes, plane_size, head_devices...  64.1 us
    unnamed x1, local copies, waits for them, and re-layouts  1.53 us

profile of v4, /device:TPU:1, one launch (start us, length us, event | category | flops | bytes accessed | tf_op | source)
XLA Modules:
  0.0 65.6 jit_solution(2802500352728383835)
XLA Ops:
  0.0 64.1 %shard_map.109 = bf16[80,512]{1,0:T(8,128)(2,1)} custom-call(bf16[80,2048]{1,0:T(8,128)(2,1)} %hidden_in.1, f32[1,2048]{1,0:T(1,128)} %bitcast.4, f32[1,2048]{1,0:T(1,128)} %bitcast.5, bf16[2048,256]{1,0:T(8,128)(2,1)} %self_query.1, bf16[2048,256]{1,0:T(8,128)(2,1)} %self_key.1, bf16[2048,256]{1,0:T(8,128)(2,1)} %self_value.1, ...), custom_call_target="tpu_custom_call" | custom-call | tf_op jit(solution)/shard_map/pallas_call | solution.py:678
  64.1 1.5 %copy.13 = bf16[80,512]{1,0:T(8,128)(2,1)} copy(bf16[80,512]{1,0:T(8,128)(2,1)} %shard_map.109) | data formatting | bytes 163840

commit v5 on v4

--- a/solution.py
+++ b/solution.py
@@ -523,6 +523,10 @@
     )
     attn_self[head] = (mixed / spread(total, hc)).astype(jnp.bfloat16)
 
+    farthest_first = sorted(
+        range(1, head_devices), key=lambda step: -min(step, head_devices - step)
+    )
+
     def exchange(buffer, send, recv):
         def copy(slot, step):
             return remote(
@@ -534,7 +538,8 @@
             )
 
         def start():
-            each(1, head_devices, lambda step: copy(head, step).start())
+            for step in farthest_first:
+                copy(head, step).start()
 
         def finish(step):
             copy(head_at(step), step).wait_recv()
@@ -556,7 +561,7 @@
         return matmul(attn_self[other], out_weights[other].reshape(share, hc), NT)
 
     mixed = hidden[:, columns].astype(jnp.float32) + self_term(0)
-    for step in range(1, head_devices):
+    for step in reversed(farthest_first):
         self_finish(step)
         mixed = mixed + self_term(step)
     mixed_rows[...] = mixed
@@ -589,7 +594,7 @@
             (ctx, other),
         )
 
-    for step in range(1, head_devices):
+    for step in farthest_first:
         query_terms[head_at(step)] = query_term(head_at(step)).astype(jnp.bfloat16)
         term_copy(step, head).start()
     cross_q = query_term(head)
@@ -617,7 +622,7 @@
     last_pair.finish()
 
     result = mixed_rows[...]
-    for step in range(head_devices):
+    for step in [0, *reversed(farthest_first)]:
         if step:
             cross_finish(step)
         other = head_at(step)

time: 65.8 us -> 65 us (0.988)
  Pallas kernels: 64.1 us -> 63 us
    pallas_call x1, Pallas kernels: 64.1 us -> 63 us  [body(): pl.pallas_call(functools.partial(kernel, planes, plane_size, head_devices...]
where the time goes in v5:
time: 65 us; the launch traced here: 64.6 us
  Pallas kernels  63 us (97%)
  local copies, waits for them, and re-layouts  1.53 us (2%)
    pallas_call x1, Pallas kernels, body(): pl.pallas_call(functools.partial(kernel, planes, plane_size, head_devices...  63 us
    unnamed x1, local copies, waits for them, and re-layouts  1.53 us

profile of v5, /device:TPU:1, one launch (start us, length us, event | category | flops | bytes accessed | tf_op | source)
XLA Modules:
  0.0 64.6 jit_solution(15499805611790197613)
XLA Ops:
  0.0 63.0 %shard_map.109 = bf16[80,512]{1,0:T(8,128)(2,1)} custom-call(bf16[80,2048]{1,0:T(8,128)(2,1)} %hidden_in.1, f32[1,2048]{1,0:T(1,128)} %bitcast.4, f32[1,2048]{1,0:T(1,128)} %bitcast.5, bf16[2048,256]{1,0:T(8,128)(2,1)} %self_query.1, bf16[2048,256]{1,0:T(8,128)(2,1)} %self_key.1, bf16[2048,256]{1,0:T(8,128)(2,1)} %self_value.1, ...), custom_call_target="tpu_custom_call" | custom-call | tf_op jit(solution)/shard_map/pallas_call | solution.py:683
  63.0 1.5 %copy.13 = bf16[80,512]{1,0:T(8,128)(2,1)} copy(bf16[80,512]{1,0:T(8,128)(2,1)} %shard_map.109) | data formatting | bytes 163840

commit v6 on v5

--- a/solution.py
+++ b/solution.py
@@ -104,7 +104,8 @@
         copy(slot, sender, partner).start()
 
     def to_line(slot, sender):
-        each(1, x_size, lambda step: copy(slot, sender + step, device_of(slot_at(step, l))).start())
+        for step in sorted(range(1, x_size), key=lambda step: -min(step, x_size - step)):
+            copy(slot, sender + step, device_of(slot_at(step, l))).start()
 
     class Gather:
         @staticmethod

time: 65 us -> 64.7 us (level)
  no operation moved by 1% of the time
where the time goes in v6:
time: 64.7 us; the launch traced here: 64.4 us
  Pallas kernels  62.8 us (97%)
  local copies, waits for them, and re-layouts  1.53 us (2%)
    pallas_call x1, Pallas kernels, body(): pl.pallas_call(functools.partial(kernel, planes, plane_size, head_devices...  62.8 us
    unnamed x1, local copies, waits for them, and re-layouts  1.53 us

profile of v6, /device:TPU:1, one launch (start us, length us, event | category | flops | bytes accessed | tf_op | source)
XLA Modules:
  0.0 64.4 jit_solution(767815663150113364)
XLA Ops:
  0.0 62.8 %shard_map.109 = bf16[80,512]{1,0:T(8,128)(2,1)} custom-call(bf16[80,2048]{1,0:T(8,128)(2,1)} %hidden_in.1, f32[1,2048]{1,0:T(1,128)} %bitcast.4, f32[1,2048]{1,0:T(1,128)} %bitcast.5, bf16[2048,256]{1,0:T(8,128)(2,1)} %self_query.1, bf16[2048,256]{1,0:T(8,128)(2,1)} %self_key.1, bf16[2048,256]{1,0:T(8,128)(2,1)} %self_value.1, ...), custom_call_target="tpu_custom_call" | custom-call | tf_op jit(solution)/shard_map/pallas_call | solution.py:684
  62.8 1.5 %copy.13 = bf16[80,512]{1,0:T(8,128)(2,1)} copy(bf16[80,512]{1,0:T(8,128)(2,1)} %shard_map.109) | data formatting | bytes 163840
